TPU v7x, 32 devices: a whole 2x2x4 slice. The times are simulated.
32 devices in a mesh: gx: 4 (over z), gy: 8 (over y, x, core).
Axes of the slice: x: 2, y: 2, z: 4, core: 2. Of those that a mesh axis runs over, the one named last changes fastest.
Arguments:
- orbitals: float32 [2, 128, 128, 256], P(None, 'gx', 'gy'), may hold values from -6 to 6
- potential: float32 [128, 128, 256], P('gx', 'gy'), may hold values from -4 to 4
- projectors: float32 [1024, 9, 1024], P(('gx', 'gy')), may hold values from -3 to 3
- strengths: float32 [9], replicated, may hold values from 0.5 to 2
- atom_owner: int32 [640], replicated, may hold values from 0 to 31, as said below
- slot_atom: int32 [1024], P(('gx', 'gy')), may hold values from 0 to 640, as said below
- slot_offset: int32 [3, 1024], P(None, ('gx', 'gy')), may hold values from 0 to 240, as said below
Outputs:
- first_filter: float32 [2, 128, 128, 256], P(None, 'gx', 'gy')
- second_filter: float32 [2, 128, 128, 256], P(None, 'gx', 'gy')
Inputs may be any that keep to these rules, and one draw needn't show every extreme that they name: `atom_owner`: every tile owns 1 to 39 atoms, and some tile owns exactly 39. `slot_atom`: every live slot is linked; the first slots of a tile are live and the rest empty; at most 32 live slots a tile, and some tile has empty slots. `slot_offset`: A patch lies within its tile: the first entry is at most 24, the second at most 8, the third at most 240, which some slot reaches.
All inputs are finite; a program needn't handle non-finite values.
Results may differ from a plain program's by a relative error of at most 0.00012.
Values sent between devices are 32-bit elements; how exact they have to be, the bound alone decides.
A program may use at most 64 MiB of HBM per device.

v0:
```python
import functools

import jax
import jax.numpy as jnp
from jax import lax
from jax.experimental import pallas as pl
from jax.experimental.pallas import tpu as pltpu
from jax.sharding import PartitionSpec as P

BXY = 8
BZ = 16
HALO = 6
GROUP = 4
MESH = pl.DeviceIdType.MESH
HIGHEST = lax.Precision.HIGHEST

LAPLACE_COEFFS = (
    -5369.0 / 1800.0,
    12.0 / 7.0,
    -15.0 / 56.0,
    10.0 / 189.0,
    -1.0 / 112.0,
    2.0 / 1925.0,
    -1.0 / 16632.0,
)
SPACING = 0.4
CENTER = 45.0
HALF_WIDTH = 48.0
KINETIC = -0.5 / (SPACING * SPACING)
VMEM_LIMIT = 40 * 1024 * 1024


def lane_windows(start):
    lanes = lax.broadcasted_iota(jnp.int32, (BXY, 128), 1)
    return [(lanes + h * 128 >= start) & (lanes + h * 128 < start + BZ) for h in range(2)]


def gather_partials(field_b, packed, offset, atom_row, sums, msg):
    slots, nproj = packed.shape[0], packed.shape[1]
    size_x = field_b.shape[2] // 2
    quantities = 2 * nproj
    rows = sums.shape[0]
    sums[quantities * slots :, :] = jnp.zeros((rows - quantities * slots, 128), jnp.float32)

    def body(s, _):
        x0, y0, z0 = offset[0, s], offset[1, s], offset[2, s]
        windows = lane_windows(z0)
        patches = []
        for o in range(2):
            total = None
            for b in range(BXY):
                rows = pl.ds(o * size_x + x0, BXY)
                plane = jnp.where(windows[0], field_b[y0 + b, 0, rows, :], 0.0)
                plane = jnp.where(windows[1], field_b[y0 + b, 1, rows, :], plane)
                plane = pltpu.roll(plane, (b * BZ + 256 - z0) & 127, 1)
                total = plane if total is None else total + plane
            patches.append(total)
        for p in range(nproj):
            values = packed[s, p]
            for o in range(2):
                row = jnp.sum(values * patches[o], axis=0, keepdims=True)
                sums[pl.ds((2 * p + o) * slots + s, 1), :] = row
        return 0

    lax.fori_loop(0, slots, body, 0, unroll=2)
    summed = lax.dot_general(
        jnp.ones((8, 128), jnp.float32),
        sums[...],
        (((1,), (1,)), ((), ())),
        precision=HIGHEST,
        preferred_element_type=jnp.float32,
    )
    row_ids = lax.broadcasted_iota(jnp.int32, (8, 128), 0)
    out = jnp.where(row_ids == 5, atom_row[...], 0.0)
    for r in range(5):
        out = jnp.where(row_ids == r, summed[:, r * 128 : (r + 1) * 128], out)
    msg[...] = out


def scatter_added(field_b, packed, offset, coef, strengths, scale):
    slots, nproj = packed.shape[0], packed.shape[1]
    size_x = field_b.shape[2] // 2

    def body(s, _):
        x0, y0, z0 = offset[0, s], offset[1, s], offset[2, s]
        windows = lane_windows(z0)
        added = [None, None]
        for p in range(nproj):
            values = packed[s, p]
            for o in range(2):
                q = 2 * p + o
                factor = coef[q // GROUP, (q % GROUP) * slots + s] * (strengths[0, p] * scale)
                term = values * factor
                added[o] = term if added[o] is None else added[o] + term
        for o in range(2):
            for b in range(BXY):
                moved = pltpu.roll(added[o], (z0 + 128 - b * BZ) & 127, 1)
                for h in range(2):
                    where = (y0 + b, h, pl.ds(o * size_x + x0, BXY), slice(None))
                    field_b[where] = field_b[where] + jnp.where(windows[h], moved, 0.0)
        return 0

    lax.fori_loop(0, slots, body, 0)


def first_kernel(orb, proj, atom_row, offset, field_b, packed, msg, sums):
    size_x, size_y = orb.shape[1], orb.shape[2]
    for o in range(2):
        for x in range(0, size_x, 8):
            turned = jnp.swapaxes(orb[o, x : x + 8], 0, 1)
            for h in range(2):
                rows = slice(o * size_x + x, o * size_x + x + 8)
                field_b[:, h, rows, :] = turned[:, :, h * 128 : (h + 1) * 128]
    slots = proj.shape[0]

    def pack(s, _):
        for a in range(BXY):
            packed[s, :, a, :] = proj[s, :, a * 128 : (a + 1) * 128]
        return 0

    lax.fori_loop(0, slots, pack, 0)
    gather_partials(field_b, packed, offset, atom_row, sums, msg)


def middle_kernel(
    base_a, base_b, packed, atom_row, offset, coef, strengths, out_a, out_b, msg, sums, *, scale
):
    size_x = base_a.shape[1]
    out_b[...] = base_b[...]
    scatter_added(out_b, packed, offset, coef, strengths, scale)
    for o in range(2):
        for x in range(0, size_x, 8):
            rows = slice(o * size_x + x, o * size_x + x + 8)
            for h in range(2):
                lanes = slice(h * 128, (h + 1) * 128)
                block = base_a[o, x : x + 8, :, lanes] + jnp.swapaxes(out_b[:, h, rows, :], 0, 1)
                out_a[o, x : x + 8, :, lanes] = block
                out_b[:, h, rows, :] = jnp.swapaxes(block, 0, 1)
    gather_partials(out_b, packed, offset, atom_row, sums, msg)


def last_kernel(base_a, base_b, packed, offset, coef, strengths, out_a, work, *, scale):
    size_x = base_a.shape[1]
    work[...] = base_b[...]
    scatter_added(work, packed, offset, coef, strengths, scale)
    for o in range(2):
        for x in range(0, size_x, 8):
            rows = slice(o * size_x + x, o * size_x + x + 8)
            for h in range(2):
                lanes = slice(h * 128, (h + 1) * 128)
                block = base_a[o, x : x + 8, :, lanes] + jnp.swapaxes(work[:, h, rows, :], 0, 1)
                out_a[o, x : x + 8, :, lanes] = block


def partner_offsets(devices):
    if devices >= 5:
        return (0, 1, 2, devices - 2, devices - 1)
    return tuple(range(devices))


def exchange_kernel(*refs, scale, subtract, grid_x, grid_y):
    if subtract:
        field, field_b, pot, msg, atom_col, previous = refs[:6]
        refs = refs[6:]
    else:
        field, field_b, pot, msg, atom_col = refs[:5]
        refs = refs[5:]
    base_a, base_b, coef, pad_a, pad_b, inbox, halo_send, halo_recv, msg_send, msg_recv = refs
    size_x, size_y, depth = field.shape[1], field.shape[2], field.shape[3]
    me_x, me_y = lax.axis_index("gx"), lax.axis_index("gy")
    steps = [
        (dx, dy)
        for dx in partner_offsets(grid_x)
        for dy in partner_offsets(grid_y)
        if (dx, dy) != (0, 0)
    ]

    def device(dx, dy):
        return (lax.rem(me_x + dx, grid_x), lax.rem(me_y + dy, grid_y))

    barrier = pltpu.get_barrier_semaphore()
    for dx, dy in steps:
        pl.semaphore_signal(barrier, inc=1, device_id=device(dx, dy), device_id_type=MESH)
    pl.semaphore_wait(barrier, len(steps))

    halos = []
    for i, (src, dst, target) in enumerate(
        (
            (
                field_b.at[pl.ds(size_y - HALO, HALO)],
                pad_b.at[pl.ds(0, HALO)],
                device(0, 1),
            ),
            (
                field_b.at[pl.ds(0, HALO)],
                pad_b.at[pl.ds(HALO + size_y, HALO)],
                device(0, grid_y - 1),
            ),
            (
                field.at[:, pl.ds(size_x - HALO, HALO)],
                pad_a.at[:, pl.ds(0, HALO)],
                device(1, 0),
            ),
            (
                field.at[:, pl.ds(0, HALO)],
                pad_a.at[:, pl.ds(HALO + size_x, HALO)],
                device(grid_x - 1, 0),
            ),
        )
    ):
        halos.append(
            pltpu.make_async_remote_copy(
                src_ref=src,
                dst_ref=dst,
                send_sem=halo_send.at[i],
                recv_sem=halo_recv.at[i],
                device_id=target,
                device_id_type=MESH,
            )
        )
    letters = []
    for i, (dx, dy) in enumerate(steps):
        letters.append(
            pltpu.make_async_remote_copy(
                src_ref=msg,
                dst_ref=inbox.at[i],
                send_sem=msg_send.at[i],
                recv_sem=msg_recv.at[i],
                device_id=device(dx, dy),
                device_id_type=MESH,
            )
        )
    for copy in halos:
        copy.start()
    for copy in letters:
        copy.start()

    factor = KINETIC * scale
    row = lax.broadcasted_iota(jnp.int32, (depth, depth), 0)
    column = lax.broadcasted_iota(jnp.int32, (depth, depth), 1)
    apart = jnp.abs(row - column)
    band = jnp.where(apart == 0, 3.0 * LAPLACE_COEFFS[0] * factor - CENTER * scale, 0.0)
    for reach in range(1, HALO + 1):
        band = jnp.where(apart == reach, LAPLACE_COEFFS[reach] * factor, band)
    width = 8

    def own(i, _):
        xs = pl.ds(i * width, width)
        local = pot[xs] * scale
        for o in range(2):
            block = field[o, xs]
            along_z = lax.dot_general(
                block.reshape(width * size_y, depth),
                band,
                (((1,), (0,)), ((), ())),
                precision=HIGHEST,
                preferred_element_type=jnp.float32,
            ).reshape(width, size_y, depth)
            total = along_z + local * block
            if subtract:
                total = total - previous[o, xs]
            base_a[o, xs] = total
            pad_a[o, pl.ds(HALO + i * width, width)] = block
        return 0

    lax.fori_loop(0, size_x // width, own, 0)
    pad_b[HALO : HALO + size_y] = field_b[...]

    group_r = lax.broadcasted_iota(jnp.int32, (128, 128), 0) // 32
    group_c = lax.broadcasted_iota(jnp.int32, (128, 128), 1) // 32
    same_group = group_r == group_c
    mine = atom_col[...]

    def matched(letter):
        same = same_group & (mine == letter[5:6, :])
        return lax.dot_general(
            letter,
            same.astype(jnp.float32),
            (((1,), (1,)), ((), ())),
            precision=HIGHEST,
            preferred_element_type=jnp.float32,
        )

    for copy in letters:
        copy.wait()
    coef[...] = matched(msg[...])

    def add_letter(i, _):
        coef[...] = coef[...] + matched(inbox[i])
        return 0

    lax.fori_loop(0, len(steps), add_letter, 0)

    for copy in halos[2:]:
        copy.wait()

    def along_x(x, _):
        for o in range(2):
            total = base_a[o, x]
            for reach in range(1, HALO + 1):
                pair = pad_a[o, x + HALO + reach] + pad_a[o, x + HALO - reach]
                total = total + (LAPLACE_COEFFS[reach] * factor) * pair
            base_a[o, x] = total
        return 0

    lax.fori_loop(0, size_x, along_x, 0)
    for copy in halos[:2]:
        copy.wait()

    def along_y(y, _):
        for h in range(2):
            total = None
            for reach in range(1, HALO + 1):
                pair = pad_b[y + HALO + reach, h] + pad_b[y + HALO - reach, h]
                term = (LAPLACE_COEFFS[reach] * factor) * pair
                total = term if total is None else total + term
            base_b[y, h] = total
        return 0

    lax.fori_loop(0, size_y, along_y, 0)


def shards(
    orbitals, potential, projectors, strengths, atom_owner, slot_atom, slot_offset, grid_x, grid_y
):
    orbit, size_x, size_y, depth = orbitals.shape
    slots, nproj, box = projectors.shape
    f32 = jnp.float32
    vmem = pl.BlockSpec(memory_space=pltpu.VMEM)
    smem = pl.BlockSpec(memory_space=pltpu.SMEM)
    shape_a = jax.ShapeDtypeStruct(orbitals.shape, f32)
    shape_b = jax.ShapeDtypeStruct((size_y, 2, orbit * size_x, depth // 2), f32)
    shape_p = jax.ShapeDtypeStruct((slots, nproj, BXY, 128), f32)
    shape_m = jax.ShapeDtypeStruct((8, 128), f32)
    sums = pltpu.VMEM((20 * slots, 128), f32)

    live = slot_atom < atom_owner.shape[0]
    numbers = slot_atom.astype(f32)
    atom_row = jnp.tile(jnp.where(live, numbers, -1.0), GROUP)
    atom_row = jnp.broadcast_to(atom_row[None, :], (8, 128))
    atom_col = jnp.tile(jnp.where(live, numbers, -2.0), GROUP)
    atom_col = jnp.broadcast_to(atom_col[:, None], (128, 128))
    strengths = strengths.reshape(1, nproj)
    plain = pltpu.CompilerParams(vmem_limit_bytes=VMEM_LIMIT)

    field_b, packed, msg = pl.pallas_call(
        first_kernel,
        out_shape=(shape_b, shape_p, shape_m),
        in_specs=[vmem, vmem, vmem, smem],
        out_specs=(vmem, vmem, vmem),
        scratch_shapes=[sums],
        compiler_params=plain,
        name="gather_partials",
    )(orbitals, projectors, atom_row, slot_offset)

    steps = len(partner_offsets(grid_x)) * len(partner_offsets(grid_y)) - 1

    def exchange(field, field_b, msg, previous, scale, number):
        args = [field, field_b, potential, msg, atom_col]
        if previous is not None:
            args.append(previous)
        return pl.pallas_call(
            functools.partial(
                exchange_kernel,
                scale=scale,
                subtract=previous is not None,
                grid_x=grid_x,
                grid_y=grid_y,
            ),
            out_shape=(shape_a, shape_b, shape_m),
            in_specs=[vmem] * len(args),
            out_specs=(vmem, vmem, vmem),
            scratch_shapes=[
                pltpu.VMEM((orbit, size_x + 2 * HALO, size_y, depth), f32),
                pltpu.VMEM((size_y + 2 * HALO, 2, orbit * size_x, depth // 2), f32),
                pltpu.VMEM((steps, 8, 128), f32),
                pltpu.SemaphoreType.DMA((4,)),
                pltpu.SemaphoreType.DMA((4,)),
                pltpu.SemaphoreType.DMA((steps,)),
                pltpu.SemaphoreType.DMA((steps,)),
            ],
            compiler_params=pltpu.CompilerParams(
                collective_id=number, has_side_effects=True, vmem_limit_bytes=VMEM_LIMIT
            ),
            name="exchange_%d" % number,
        )(*args)

    base_a, base_b, coef = exchange(orbitals, field_b, msg, None, 1.0 / HALF_WIDTH, 0)
    first, field_b, msg = pl.pallas_call(
        functools.partial(middle_kernel, scale=1.0 / HALF_WIDTH),
        out_shape=(shape_a, shape_b, shape_m),
        in_specs=[vmem, vmem, vmem, vmem, smem, smem, smem],
        out_specs=(vmem, vmem, vmem),
        scratch_shapes=[sums],
        compiler_params=plain,
        name="scatter_gather",
    )(base_a, base_b, packed, atom_row, slot_offset, coef, strengths)
    base_a, base_b, coef = exchange(first, field_b, msg, orbitals, 2.0 / HALF_WIDTH, 1)
    second = pl.pallas_call(
        functools.partial(last_kernel, scale=2.0 / HALF_WIDTH),
        out_shape=shape_a,
        in_specs=[vmem, vmem, vmem, smem, smem, smem],
        out_specs=vmem,
        scratch_shapes=[pltpu.VMEM((size_y, 2, orbit * size_x, depth // 2), f32)],
        compiler_params=plain,
        name="scatter_last",
    )(base_a, base_b, packed, slot_offset, coef, strengths)
    return (first, second)


def solution(mesh):
    return jax.shard_map(
        functools.partial(shards, grid_x=mesh.shape["gx"], grid_y=mesh.shape["gy"]),
        mesh=mesh,
        in_specs=(
            P(None, "gx", "gy", None),
            P("gx", "gy", None),
            P(("gx", "gy"), None, None),
            P(),
            P(),
            P(("gx", "gy")),
            P(None, ("gx", "gy")),
        ),
        out_specs=(P(None, "gx", "gy", None), P(None, "gx", "gy", None)),
        check_vma=False,
    )
```

profile of v0, /device:TPU:0, one launch (start us, length us, event | category | flops | bytes accessed | tf_op | source)
XLA Modules:
  0.0 70.5 jit_solution(17876118264886435108)
XLA Ops:
  0.6 0.7 %compare_select_fusion = (f32[32]{0:T(128)S(1)}, f32[32]{0:T(128)S(1)}) fusion(s32[32]{0:T(128)} %param.11), kind=kLoop, calls=%fused_computation | loop fusion | flops 128 | bytes 384 | tf_op jit(solution)/shard_map/jit(_where)/select_n | solution.py:341
  1.4 0.1 broadcast_in_dim.25
  1.5 0.1 broadcast_in_dim.22
  1.5 0.1 broadcast_in_dim.26.refs_4_
  1.6 0.0 copy-start
  1.6 0.0 copy-start.3
  1.6 2.1 %copy.8.proj = f32[32,9,1024]{2,1,0:T(8,128)S(1)} copy(f32[32,9,1024]{2,0,1:T(8,128)} %param.9) | data formatting | bytes 2359296 | tf_op args[2]
  3.8 0.0 copy-done
  3.8 0.0 copy-done.3
  3.8 0.0 copy-start.1
  3.8 4.4 %gather_partials.1 = (f32[16,2,64,128]{3,2,1,0:T(8,128)S(1)}, f32[32,9,8,128]{3,2,1,0:T(8,128)S(1)}, f32[8,128]{1,0:T(8,128)S(1)}) custom-call(f32[2,32,16,256]{3,2,1,0:T(8,128)S(1)} %copy-done, f32[32,9,1024]{2,1,0:T(8,128)S(1)} %copy.8.proj, f32[8,128]{1,0:T(8,128)S(1)} %broadcast_in_dim.23.atom_row, s32[3,32]{1,0:T(4,128)S(1)} %copy-done.3), custom_call_target="tpu_custom_call" | custom-call | tf_op jit(solution)/shard_map/gather_partials/pallas_call | solution.py:346
  8.1 0.0 copy-done.1
  8.2 0.0 copy-start.4
  8.2 24.7 %exchange_0.1 = (f32[2,32,16,256]{3,2,1,0:T(8,128)S(1)}, f32[16,2,64,128]{3,2,1,0:T(8,128)S(1)}, f32[8,128]{1,0:T(8,128)S(1)}) custom-call(f32[2,32,16,256]{3,2,1,0:T(8,128)S(1)} %copy-done, f32[16,2,64,128]{3,2,1,0:T(8,128)S(1)} %get-tuple-element.14.refs_1_, f32[32,16,256]{2,1,0:T(8,128)S(1)} %copy-done.1, f32[8,128]{1,0:T(8,128)S(1)} %get-tuple-element.15.refs_3_, ...), custom_call_target="tpu_custom_call" | custom-call | tf_op jit(solution)/shard_map/exchange_0/pallas_call | solution.py:362
  32.9 0.0 copy-done.4
  32.9 8.0 %scatter_gather.1 = (f32[2,32,16,256]{3,2,1,0:T(8,128)}, f32[16,2,64,128]{3,2,1,0:T(8,128)S(1)}, f32[8,128]{1,0:T(8,128)S(1)}) custom-call(f32[2,32,16,256]{3,2,1,0:T(8,128)S(1)} %get-tuple-element.16.base_a, f32[16,2,64,128]{3,2,1,0:T(8,128)S(1)} %get-tuple-element.17.base_b, f32[32,9,8,128]{3,2,1,0:T(8,128)S(1)} %get-tuple-element.18.packed, ...), custom_call_target="tpu_custom_call" | custom-call | tf_op jit(solution)/shard_map/scatter_gather/pallas_call | solution.py:389
  40.9 0.0 copy-start.2
  40.9 1.2 %copy-done.2 = f32[2,32,16,256]{3,2,1,0:T(8,128)S(1)} copy-done((f32[2,32,16,256]{3,2,1,0:T(8,128)S(1)}, f32[2,32,16,256]{3,2,1,0:T(8,128)}, u32[]{:S(2)}) %copy-start.2) | copy-done | bytes 1048600
  42.1 22.8 %exchange_1.1 = (f32[2,32,16,256]{3,2,1,0:T(8,128)S(1)}, f32[16,2,64,128]{3,2,1,0:T(8,128)S(1)}, f32[8,128]{1,0:T(8,128)S(1)}) custom-call(f32[2,32,16,256]{3,2,1,0:T(8,128)S(1)} %copy-done.2, f32[16,2,64,128]{3,2,1,0:T(8,128)S(1)} %get-tuple-element.21.refs_1_, f32[32,16,256]{2,1,0:T(8,128)S(1)} %copy-done.1, f32[8,128]{1,0:T(8,128)S(1)} %get-tuple-element.22.refs_3_, ...), custom_call_target="tpu_custom_call" | custom-call | tf_op jit(solution)/shard_map/exchange_1/pallas_call | solution.py:362
  64.9 5.6 %scatter_last.1 = f32[2,32,16,256]{3,2,1,0:T(8,128)} custom-call(f32[2,32,16,256]{3,2,1,0:T(8,128)S(1)} %get-tuple-element.23.base_a, f32[16,2,64,128]{3,2,1,0:T(8,128)S(1)} %get-tuple-element.24.base_b, f32[32,9,8,128]{3,2,1,0:T(8,128)S(1)} %get-tuple-element.18.packed, s32[3,32]{1,0:T(4,128)S(1)} %copy-done.3, f32[8,128]{1,0:T(8,128)S(1)} %get-tuple-element.25.coef, ...), custom_call_target="tpu_custom_call" | custom-call | tf_op jit(solution)/shard_map/scatter_last/pallas_call | solution.py:399
  (3 shorter events, 0.0 us)
Async XLA Ops:
  1.6 2.1 %copy-start = (f32[2,32,16,256]{3,2,1,0:T(8,128)S(1)}, f32[2,32,16,256]{3,2,1,0:T(8,128)}, u32[]{:S(2)}) copy-start(f32[2,32,16,256]{3,2,1,0:T(8,128)} %refs_5_.1) | copy-start | bytes 3145732
  1.6 2.1 %copy-start.3 = (s32[3,32]{1,0:T(4,128)S(1)}, s32[3,32]{1,0:T(4,128)}, u32[]{:S(2)}) copy-start(s32[3,32]{1,0:T(4,128)} %offset.5) | copy-start | bytes 1156
  3.8 4.4 %copy-start.1 = (f32[32,16,256]{2,1,0:T(8,128)S(1)}, f32[32,16,256]{2,1,0:T(8,128)}, u32[]{:S(2)}) copy-start(f32[32,16,256]{2,1,0:T(8,128)} %refs_2_.3) | copy-start | bytes 1572868
  8.2 24.7 %copy-start.4 = (f32[9]{0:T(128)S(1)}, f32[9]{0:T(128)}, u32[]{:S(2)}) copy-start(f32[9]{0:T(128)} %param.10) | copy-start | bytes 112
  40.9 1.2 %copy-start.2 = (f32[2,32,16,256]{3,2,1,0:T(8,128)S(1)}, f32[2,32,16,256]{3,2,1,0:T(8,128)}, u32[]{:S(2)}) copy-start(f32[2,32,16,256]{3,2,1,0:T(8,128)} %get-tuple-element.12.refs_0_) | copy-start | bytes 3145732
where the time goes:
time: 70.7 us; the launch traced here: 70.5 us
  Pallas kernels  65.4 us (93%)
  local copies, waits for them, and re-layouts  3.6 us (5%)
  other arithmetic  0.73 us (1%)
  between operations  0.71 us (1%)
    pallas_call x2, Pallas kernels, exchange(): pl.pallas_call(functools.partial(exchange_kernel, scale=scale, subtract=p...  47.5 us
    pallas_call x1, Pallas kernels, shards(): pl.pallas_call(functools.partial(middle_kernel, scale=1.0 / HALF_WIDTH),...  7.96 us
    pallas_call x1, Pallas kernels, shards(): pl.pallas_call(functools.partial(last_kernel, scale=2.0 / HALF_WIDTH), ou...  5.58 us
    pallas_call x1, Pallas kernels, shards(): pl.pallas_call(first_kernel, out_shape=(shape_b, shape_p, shape_m), in_sp...  4.36 us
    unnamed x11, local copies, waits for them, and re-layouts  3.35 us

commit v1 on v0

--- a/solution.py
+++ b/solution.py
@@ -55,11 +55,13 @@
                 plane = pltpu.roll(plane, (b * BZ + 256 - z0) & 127, 1)
                 total = plane if total is None else total + plane
             patches.append(total)
+        found = []
         for p in range(nproj):
             values = packed[s, p]
             for o in range(2):
-                row = jnp.sum(values * patches[o], axis=0, keepdims=True)
-                sums[pl.ds((2 * p + o) * slots + s, 1), :] = row
+                found.append(jnp.sum(values * patches[o], axis=0, keepdims=True))
+        for q, row in enumerate(found):
+            sums[pl.ds(q * slots + s, 1), :] = row
         return 0
 
     lax.fori_loop(0, slots, body, 0, unroll=2)
@@ -92,15 +94,26 @@
                 factor = coef[q // GROUP, (q % GROUP) * slots + s] * (strengths[0, p] * scale)
                 term = values * factor
                 added[o] = term if added[o] is None else added[o] + term
-        for o in range(2):
-            for b in range(BXY):
-                moved = pltpu.roll(added[o], (z0 + 128 - b * BZ) & 127, 1)
-                for h in range(2):
-                    where = (y0 + b, h, pl.ds(o * size_x + x0, BXY), slice(None))
-                    field_b[where] = field_b[where] + jnp.where(windows[h], moved, 0.0)
-        return 0
-
-    lax.fori_loop(0, slots, body, 0)
+        places = [
+            (o, b, h, (y0 + b, h, pl.ds(o * size_x + x0, BXY), slice(None)))
+            for o in range(2)
+            for b in range(BXY)
+            for h in range(2)
+        ]
+        before = [field_b[where] for _, _, _, where in places]
+        moved = [
+            [pltpu.roll(added[o], (z0 + 128 - b * BZ) & 127, 1) for b in range(BXY)]
+            for o in range(2)
+        ]
+        after = [
+            old + jnp.where(windows[h], moved[o][b], 0.0)
+            for old, (o, b, h, _) in zip(before, places)
+        ]
+        for value, (_, _, _, where) in zip(after, places):
+            field_b[where] = value
+        return 0
+
+    lax.fori_loop(0, slots, body, 0, unroll=2)
 
 
 def first_kernel(orb, proj, atom_row, offset, field_b, packed, msg, sums):
@@ -230,9 +243,9 @@
                 device_id_type=MESH,
             )
         )
+    for copy in letters:
+        copy.start()
     for copy in halos:
-        copy.start()
-    for copy in letters:
         copy.start()
 
     factor = KINETIC * scale
@@ -273,26 +286,16 @@
 
     def matched(letter):
         same = same_group & (mine == letter[5:6, :])
+        high = letter.astype(jnp.bfloat16).astype(jnp.float32)
+        rest = letter - high
+        middle = rest.astype(jnp.bfloat16).astype(jnp.float32)
+        terms = jnp.concatenate([high, middle, rest - middle, jnp.zeros_like(letter)], axis=0)
         return lax.dot_general(
-            letter,
-            same.astype(jnp.float32),
+            terms.astype(jnp.bfloat16),
+            jnp.where(same, 1.0, 0.0).astype(jnp.bfloat16),
             (((1,), (1,)), ((), ())),
-            precision=HIGHEST,
             preferred_element_type=jnp.float32,
         )
-
-    for copy in letters:
-        copy.wait()
-    coef[...] = matched(msg[...])
-
-    def add_letter(i, _):
-        coef[...] = coef[...] + matched(inbox[i])
-        return 0
-
-    lax.fori_loop(0, len(steps), add_letter, 0)
-
-    for copy in halos[2:]:
-        copy.wait()
 
     def along_x(x, _):
         for o in range(2):
@@ -302,10 +305,6 @@
                 total = total + (LAPLACE_COEFFS[reach] * factor) * pair
             base_a[o, x] = total
         return 0
-
-    lax.fori_loop(0, size_x, along_x, 0)
-    for copy in halos[:2]:
-        copy.wait()
 
     def along_y(y, _):
         for h in range(2):
@@ -317,7 +316,24 @@
             base_b[y, h] = total
         return 0
 
-    lax.fori_loop(0, size_y, along_y, 0)
+    lax.fori_loop(HALO, size_x - HALO, along_x, 0)
+    lax.fori_loop(HALO, size_y - HALO, along_y, 0)
+
+    for copy in letters:
+        copy.wait()
+    total = matched(msg[...])
+    for i in range(len(steps)):
+        total = total + matched(inbox[i])
+    coef[...] = total[0:8] + total[8:16] + total[16:24]
+
+    halos[2].wait()
+    lax.fori_loop(0, HALO, along_x, 0)
+    halos[3].wait()
+    lax.fori_loop(size_x - HALO, size_x, along_x, 0)
+    halos[0].wait()
+    lax.fori_loop(0, HALO, along_y, 0)
+    halos[1].wait()
+    lax.fori_loop(size_y - HALO, size_y, along_y, 0)
 
 
 def shards(

time: 70.7 us -> 56.2 us (0.79)
  Pallas kernels: 65.4 us -> 51 us
    pallas_call x2, Pallas kernels: 47.5 us -> 35.7 us  [exchange(): pl.pallas_call(functools.partial(exchange_kernel, scale=scale, subtract=p...]
    pallas_call x1, Pallas kernels: 5.58 us -> 4.27 us  [shards(): pl.pallas_call(functools.partial(last_kernel, scale=2.0 / HALF_WIDTH), ou...]
    pallas_call x1, Pallas kernels: 7.96 us -> 6.65 us  [shards(): pl.pallas_call(functools.partial(middle_kernel, scale=1.0 / HALF_WIDTH),...]
where the time goes in v1:
time: 56.2 us; the launch traced here: 56 us
  Pallas kernels  51 us (91%)
  local copies, waits for them, and re-layouts  3.6 us (6%)
  other arithmetic  0.73 us (1%)
  between operations  0.71 us (1%)
    pallas_call x2, Pallas kernels, exchange(): pl.pallas_call(functools.partial(exchange_kernel, scale=scale, subtract=p...  35.7 us
    pallas_call x1, Pallas kernels, shards(): pl.pallas_call(functools.partial(middle_kernel, scale=1.0 / HALF_WIDTH),...  6.65 us
    pallas_call x1, Pallas kernels, shards(): pl.pallas_call(first_kernel, out_shape=(shape_b, shape_p, shape_m), in_sp...  4.36 us
    pallas_call x1, Pallas kernels, shards(): pl.pallas_call(functools.partial(last_kernel, scale=2.0 / HALF_WIDTH), ou...  4.27 us
    unnamed x11, local copies, waits for them, and re-layouts  3.35 us

profile of v1, /device:TPU:0, one launch (start us, length us, event | category | flops | bytes accessed | tf_op | source)
XLA Modules:
  0.0 56.0 jit_solution(7216131114453495088)
XLA Ops:
  0.6 0.7 %compare_select_fusion = (f32[32]{0:T(128)S(1)}, f32[32]{0:T(128)S(1)}) fusion(s32[32]{0:T(128)} %param.11), kind=kLoop, calls=%fused_computation | loop fusion | flops 128 | bytes 384 | tf_op jit(solution)/shard_map/jit(_where)/select_n | solution.py:357
  1.4 0.1 broadcast_in_dim.25
  1.5 0.1 broadcast_in_dim.22
  1.5 0.1 broadcast_in_dim.26.refs_4_
  1.6 0.0 copy-start
  1.6 0.0 copy-start.3
  1.6 2.1 %copy.8.proj = f32[32,9,1024]{2,1,0:T(8,128)S(1)} copy(f32[32,9,1024]{2,0,1:T(8,128)} %param.9) | data formatting | bytes 2359296 | tf_op args[2]
  3.8 0.0 copy-done
  3.8 0.0 copy-done.3
  3.8 0.0 copy-start.1
  3.8 4.4 %gather_partials.1 = (f32[16,2,64,128]{3,2,1,0:T(8,128)S(1)}, f32[32,9,8,128]{3,2,1,0:T(8,128)S(1)}, f32[8,128]{1,0:T(8,128)S(1)}) custom-call(f32[2,32,16,256]{3,2,1,0:T(8,128)S(1)} %copy-done, f32[32,9,1024]{2,1,0:T(8,128)S(1)} %copy.8.proj, f32[8,128]{1,0:T(8,128)S(1)} %broadcast_in_dim.23.atom_row, s32[3,32]{1,0:T(4,128)S(1)} %copy-done.3), custom_call_target="tpu_custom_call" | custom-call | tf_op jit(solution)/shard_map/gather_partials/pallas_call | solution.py:362
  8.2 0.0 copy-done.1
  8.2 0.0 copy-start.4
  8.2 18.8 %exchange_0.1 = (f32[2,32,16,256]{3,2,1,0:T(8,128)S(1)}, f32[16,2,64,128]{3,2,1,0:T(8,128)S(1)}, f32[8,128]{1,0:T(8,128)S(1)}) custom-call(f32[2,32,16,256]{3,2,1,0:T(8,128)S(1)} %copy-done, f32[16,2,64,128]{3,2,1,0:T(8,128)S(1)} %get-tuple-element.14.refs_1_, f32[32,16,256]{2,1,0:T(8,128)S(1)} %copy-done.1, f32[8,128]{1,0:T(8,128)S(1)} %get-tuple-element.15.refs_3_, ...), custom_call_target="tpu_custom_call" | custom-call | tf_op jit(solution)/shard_map/exchange_0/pallas_call | solution.py:378
  27.0 0.0 copy-done.4
  27.0 6.6 %scatter_gather.1 = (f32[2,32,16,256]{3,2,1,0:T(8,128)}, f32[16,2,64,128]{3,2,1,0:T(8,128)S(1)}, f32[8,128]{1,0:T(8,128)S(1)}) custom-call(f32[2,32,16,256]{3,2,1,0:T(8,128)S(1)} %get-tuple-element.16.base_a, f32[16,2,64,128]{3,2,1,0:T(8,128)S(1)} %get-tuple-element.17.base_b, f32[32,9,8,128]{3,2,1,0:T(8,128)S(1)} %get-tuple-element.18.packed, ...), custom_call_target="tpu_custom_call" | custom-call | tf_op jit(solution)/shard_map/scatter_gather/pallas_call | solution.py:405
  33.7 0.0 copy-start.2
  33.7 1.2 %copy-done.2 = f32[2,32,16,256]{3,2,1,0:T(8,128)S(1)} copy-done((f32[2,32,16,256]{3,2,1,0:T(8,128)S(1)}, f32[2,32,16,256]{3,2,1,0:T(8,128)}, u32[]{:S(2)}) %copy-start.2) | copy-done | bytes 1048600
  34.9 16.8 %exchange_1.1 = (f32[2,32,16,256]{3,2,1,0:T(8,128)S(1)}, f32[16,2,64,128]{3,2,1,0:T(8,128)S(1)}, f32[8,128]{1,0:T(8,128)S(1)}) custom-call(f32[2,32,16,256]{3,2,1,0:T(8,128)S(1)} %copy-done.2, f32[16,2,64,128]{3,2,1,0:T(8,128)S(1)} %get-tuple-element.21.refs_1_, f32[32,16,256]{2,1,0:T(8,128)S(1)} %copy-done.1, f32[8,128]{1,0:T(8,128)S(1)} %get-tuple-element.22.refs_3_, ...), custom_call_target="tpu_custom_call" | custom-call | tf_op jit(solution)/shard_map/exchange_1/pallas_call | solution.py:378
  51.7 4.3 %scatter_last.1 = f32[2,32,16,256]{3,2,1,0:T(8,128)} custom-call(f32[2,32,16,256]{3,2,1,0:T(8,128)S(1)} %get-tuple-element.23.base_a, f32[16,2,64,128]{3,2,1,0:T(8,128)S(1)} %get-tuple-element.24.base_b, f32[32,9,8,128]{3,2,1,0:T(8,128)S(1)} %get-tuple-element.18.packed, s32[3,32]{1,0:T(4,128)S(1)} %copy-done.3, f32[8,128]{1,0:T(8,128)S(1)} %get-tuple-element.25.coef, ...), custom_call_target="tpu_custom_call" | custom-call | tf_op jit(solution)/shard_map/scatter_last/pallas_call | solution.py:415
  (3 shorter events, 0.0 us)
Async XLA Ops:
  1.6 2.1 %copy-start = (f32[2,32,16,256]{3,2,1,0:T(8,128)S(1)}, f32[2,32,16,256]{3,2,1,0:T(8,128)}, u32[]{:S(2)}) copy-start(f32[2,32,16,256]{3,2,1,0:T(8,128)} %refs_5_.1) | copy-start | bytes 3145732
  1.6 2.1 %copy-start.3 = (s32[3,32]{1,0:T(4,128)S(1)}, s32[3,32]{1,0:T(4,128)}, u32[]{:S(2)}) copy-start(s32[3,32]{1,0:T(4,128)} %offset.5) | copy-start | bytes 1156
  3.8 4.4 %copy-start.1 = (f32[32,16,256]{2,1,0:T(8,128)S(1)}, f32[32,16,256]{2,1,0:T(8,128)}, u32[]{:S(2)}) copy-start(f32[32,16,256]{2,1,0:T(8,128)} %refs_2_.3) | copy-start | bytes 1572868
  8.2 18.9 %copy-start.4 = (f32[9]{0:T(128)S(1)}, f32[9]{0:T(128)}, u32[]{:S(2)}) copy-start(f32[9]{0:T(128)} %param.10) | copy-start | bytes 112
  33.7 1.2 %copy-start.2 = (f32[2,32,16,256]{3,2,1,0:T(8,128)S(1)}, f32[2,32,16,256]{3,2,1,0:T(8,128)}, u32[]{:S(2)}) copy-start(f32[2,32,16,256]{3,2,1,0:T(8,128)} %get-tuple-element.12.refs_0_) | copy-start | bytes 3145732
